TPU v7x, 32 devices: a whole 2x2x4 slice. The times are simulated.
32 devices in a mesh: cohort: 4 (over y, x), dev: 8 (over z, core).
Axes of the slice: x: 2, y: 2, z: 4, core: 2. Of those that a mesh axis runs over, the one named last changes fastest.
Arguments:
- dosage: bfloat16 [65536, 2048], P(('cohort', 'dev')), may hold values from 0 to 2
- allele_freq: float32 [2048], replicated, may hold values from 0.05 to 0.5
- probes: bfloat16 [2048, 512], replicated, may hold values from -6 to 6
- owner_perm: int32 [2048], replicated, may hold values from 0 to 2047, each once
Outputs:
- projected: float32 [2048, 512], P('dev')
Inputs may be any that keep to these rules, and one draw needn't show every extreme that they name: `owner_perm`: each SNP appears exactly once.
All inputs are finite; a program needn't handle non-finite values.
Results may differ from a plain program's by a relative error of at most 0.00044.
Values sent between devices are 32-bit elements; how exact they have to be, the bound alone decides.
A program may use at most 128 MiB of HBM per device.

v0:
```python
import jax
import jax.numpy as jnp
from jax import lax
from jax.experimental import pallas as pl
from jax.experimental.pallas import tpu as pltpu
from jax.sharding import PartitionSpec as P

HI = lax.Precision.HIGHEST
NB = 128


def dot(a, b, ca, cb):
    return lax.dot_general(
        a, b, (((ca,), (cb,)), ((), ())), precision=HI, preferred_element_type=jnp.float32
    )


def factor_block(w_ref):
    sub = lax.broadcasted_iota(jnp.int32, (8, 1), 0)
    for p in range(NB // 8):
        lo = 8 * p
        panel = w_ref[lo : lo + 8, :]
        cols = [jnp.broadcast_to(panel[:, lo + j : lo + j + 1], (8, NB)) for j in range(8)]
        for j in range(8):
            r = lax.rsqrt(cols[j][j : j + 1, :])
            m = cols[j] * r
            for i in range(j + 1, 8):
                cols[i] = cols[i] - m * m[i : i + 1, :]
            r2 = jnp.concatenate([r, r], axis=1)
            m2 = jnp.concatenate([m, m], axis=1)
            u = panel[j : j + 1, :] * r2
            panel = jnp.where(sub == j, u, jnp.where(sub > j, panel - m2 * u, panel))
        w_ref[lo : lo + 8, :] = panel
        if lo + 8 < NB:
            base = (lo + 8) // 8 * 8
            left = panel[:, :NB]
            upd = dot(left, panel, 0, 0)
            w_ref[base:, :] = w_ref[base:, :] - upd[base:, :]


def cholesky_loop(a_ref, u_ref, inv_ref, w_ref):
    nb = a_ref.shape[0]
    eye = (
        lax.broadcasted_iota(jnp.int32, (NB, NB), 0) == lax.broadcasted_iota(jnp.int32, (NB, NB), 1)
    ).astype(jnp.float32)

    def step(b, c):
        at = pl.ds(pl.multiple_of(b * NB, NB), NB)
        w_ref[:, :NB] = a_ref[b, :, at]
        w_ref[:, NB:] = eye
        factor_block(w_ref)
        inv = w_ref[:, NB:]
        inv_ref[b] = inv
        u = dot(inv, a_ref[b], 1, 0)
        u_ref[b] = u

        def trail(i, c):
            cols = pl.ds(pl.multiple_of(i * NB, NB), NB)
            a_ref[i] = a_ref[i] - dot(u_ref[b, :, cols], u_ref[b], 0, 0)
            return c

        lax.fori_loop(b + 1, nb, trail, 0)
        return c

    lax.fori_loop(0, nb, step, 0)


def apply(h, u_ref, inv_ref):
    nb = u_ref.shape[0]
    xs = []
    for j in range(nb):
        t = h[:, j * NB : (j + 1) * NB]
        for k in range(j):
            t = t - dot(xs[k], u_ref[k, :, j * NB : (j + 1) * NB], 1, 0)
        xs.append(dot(t, inv_ref[j], 1, 1))
    return jnp.concatenate(xs, axis=1)


def chol_kernel(g_ref, u_ref, inv_ref, a_ref, w_ref):
    nb = u_ref.shape[0]
    for b in range(nb):
        a_ref[b] = g_ref[b * NB : (b + 1) * NB, :]
    cholesky_loop(a_ref, u_ref, inv_ref, w_ref)


def chol(gram):
    k = gram.shape[0]
    nb = k // NB
    return pl.pallas_call(
        chol_kernel,
        out_shape=(
            jax.ShapeDtypeStruct((nb, NB, k), jnp.float32),
            jax.ShapeDtypeStruct((nb, NB, NB), jnp.float32),
        ),
        in_specs=[pl.BlockSpec(memory_space=pltpu.VMEM)],
        out_specs=(pl.BlockSpec(memory_space=pltpu.VMEM),) * 2,
        scratch_shapes=[pltpu.VMEM((nb, NB, k), jnp.float32), pltpu.VMEM((NB, 2 * NB), jnp.float32)],
        compiler_params=pltpu.CompilerParams(vmem_limit_bytes=32 << 20),
        cost_estimate=pl.CostEstimate(flops=10**10, bytes_accessed=4 << 20, transcendentals=0),
    )(gram)


def apply_kernel(h_ref, u_ref, inv_ref, o_ref):
    o_ref[...] = apply(h_ref[...], u_ref, inv_ref)


def apply_inv(h, u, inv):
    return pl.pallas_call(
        apply_kernel,
        out_shape=jax.ShapeDtypeStruct(h.shape, jnp.float32),
        in_specs=[pl.BlockSpec(memory_space=pltpu.VMEM)] * 3,
        out_specs=pl.BlockSpec(memory_space=pltpu.VMEM),
        compiler_params=pltpu.CompilerParams(vmem_limit_bytes=32 << 20),
    )(h, u, inv)


def tdot(a, b):
    return lax.dot_general(a, b, (((0,), (0,)), ((), ())), preferred_element_type=jnp.float32)


def body(dosage, allele_freq, probes, owner_perm):
    mean_dose = 2.0 * allele_freq
    inv_spread = 1.0 / jnp.sqrt(2.0 * allele_freq * (1.0 - allele_freq))
    centered = ((dosage.astype(jnp.float32) - mean_dose[None, :]) * inv_spread[None, :]).astype(
        jnp.bfloat16
    )
    sketch = jnp.dot(centered, probes, preferred_element_type=jnp.float32)
    rounded = lax.reduce_precision(sketch, 8, 7)
    high = rounded.astype(jnp.bfloat16)
    low = (sketch - rounded).astype(jnp.bfloat16)
    cross = tdot(high, low)
    local_gram = tdot(high, high) + (cross + cross.T)
    gram = lax.psum(local_gram, ("cohort", "dev"))
    product = tdot(centered, high) + tdot(centered, low)
    product = jnp.take(product, owner_perm, axis=0)
    owned = lax.psum_scatter(product, "dev", scatter_dimension=0, tiled=True)
    owned = lax.psum(owned, "cohort")
    u, inv = chol(gram)
    return apply_inv(owned, u, inv)


def solution(mesh):
    return jax.shard_map(
        body,
        mesh=mesh,
        in_specs=(P(("cohort", "dev"), None), P(), P(), P()),
        out_specs=P("dev", None),
        check_vma=False,
    )
```

profile of v0, /device:TPU:14, one launch (start us, length us, event | category | flops | bytes accessed | tf_op | source)
XLA Modules:
  0.0 260.7 jit_solution(18296647392382779565)
XLA Ops:
  7.4 0.0 copy-start
  7.4 0.0 reduce-scatter.2.cloned.1.call-start
  7.4 0.9 compare_and_fusion
  8.2 0.7 fusion.8
  8.9 0.7 broadcast_multiply_fusion
  9.6 0.0 copy-done
  9.6 0.0 copy-start.4
  9.6 7.8 %fusion.2 = f32[2048,512]{1,0:T(8,128)S(1)} fusion(bf16[2048,512]{1,0:T(8,128)(2,1)S(1)} %copy-done, bf16[2048,2048]{1,0:T(8,128)(2,1)} %param.4, f32[2048]{0:T(1024)S(1)} %get-tuple-element.10, f32[2048]{0:T(1024)S(1)} %get-tuple-element.9), kind=kOutput, calls=%fused_computation.6 | convolution fusion | flops 4311744512 | bytes 14696448 | tf_op jit(solution)/shard_map/dot_general | solution.py:127
  17.4 0.0 copy-done.4
  17.4 0.0 copy-start.3
  17.4 4.6 %fusion = f32[2048,512]{1,0:T(8,128)S(1)} fusion(bf16[2048,2048]{1,0:T(8,128)(2,1)S(1)} %copy-done.4, f32[2048]{0:T(1024)S(1)} %get-tuple-element.10, f32[2048]{0:T(1024)S(1)} %get-tuple-element.9, f32[2048,512]{1,0:T(8,128)S(1)} %fusion.2), kind=kOutput, calls=%fused_computation.4 | convolution fusion | flops 4314890240 | bytes 16793600 | tf_op jit(solution)/shard_map/dot_general | solution.py:118
  22.0 0.0 copy-done.3
  22.0 6.1 %fusion.4 = f32[2048,512]{1,0:T(8,128)} fusion(f32[2048,512]{1,0:T(8,128)S(1)} %fusion, bf16[2048,2048]{1,0:T(8,128)(2,1)S(1)} %copy-done.4, f32[2048]{0:T(1024)S(1)} %get-tuple-element.10, f32[2048]{0:T(1024)S(1)} %get-tuple-element.9, f32[2048,512]{1,0:T(8,128)S(1)} %fusion.2), kind=kOutput, calls=%fused_computation.8 | convolution fusion | flops 4314890240 | bytes 20987904 | tf_op jit(solution)/shard_map/dot_general | solution.py:118
  28.2 11.7 %gather_fusion = f32[2048,512]{1,0:T(8,128)} fusion(f32[2048,512]{1,0:T(8,128)} %fusion.4, s32[2048]{0:T(1024)S(1)} %fusion.8), kind=kCustom, calls=%fused_computation | custom fusion | bytes 8396800 | tf_op jit(solution)/shard_map/jit(_take)/gather | solution.py:135
  39.9 3.8 %broadcast_select_fusion = f32[2048,512]{1,0:T(8,128)} fusion(f32[2048,512]{1,0:T(8,128)} %gather_fusion, pred[2048]{0:T(1024)(128)(4,1)S(1)} %compare_and_fusion), kind=kLoop, calls=%fused_computation.9 | loop fusion | flops 1048576 | bytes 8390656 | tf_op jit(solution)/shard_map/jit(_take)/select_n | solution.py:135
  43.7 0.0 reduce-scatter.2.cloned.1.call-update
  43.7 0.2 all-reduce.5.cloned.1.call-start
  43.9 4.7 %fusion.5 = f32[512,512]{1,0:T(8,128)S(1)} fusion(f32[2048,512]{1,0:T(8,128)} %copy-done.3), kind=kOutput, calls=%fused_computation.12 | convolution fusion | flops 1078984704 | bytes 5242880 | tf_op jit(solution)/shard_map/dot_general | solution.py:118
  48.7 1.3 copy.5
  50.0 6.3 %convolution_add_fusion = f32[512,512]{1,0:T(8,128)} fusion(f32[512,512]{1,0:T(8,128)S(1)} %fusion.5, f32[512,512]{0,1:T(8,128)} %copy.5, f32[2048,512]{1,0:T(8,128)} %copy-done.3), kind=kOutput, calls=%fused_computation.10 | convolution fusion | flops 1076363264 | bytes 7340032 | tf_op jit(solution)/shard_map/dot_general | solution.py:118
  56.3 0.0 all-reduce.5.cloned.1.call-update
  56.3 0.0 all-reduce.3.cloned.1.call-start
  56.4 38.7 %reduce-scatter.2.cloned.1.call-done = f32[256,512]{1,0:T(8,128)} async-done(((f32[2048,512]{1,0:T(8,128)}), f32[256,512]{1,0:T(8,128)}) %reduce-scatter.2.cloned.1.call-update) | async-done | bytes 524304 | tf_op jit(solution)/shard_map/reduce_scatter | solution.py:136
  95.1 0.0 all-reduce.3.cloned.1.call-update
  95.1 107.0 %all-reduce.5.cloned.1.call-done.g_ref = f32[512,512]{1,0:T(8,128)} async-done(((f32[512,512]{1,0:T(8,128)}), f32[512,512]{1,0:T(8,128)}) %all-reduce.5.cloned.1.call-update) | async-done | bytes 1048592 | tf_op jit(solution)/shard_map/psum | solution.py:133
  202.1 0.0 copy-start.2
  202.1 1.2 copy-done.2
  203.3 35.9 %shard_map.46 = (f32[4,128,512]{2,1,0:T(8,128)S(1)}, f32[4,128,128]{2,1,0:T(8,128)S(1)}) custom-call(f32[512,512]{1,0:T(8,128)S(1)} %copy-done.2), custom_call_target="tpu_custom_call" | custom-call | flops 10000000000 | bytes 4194304 | tf_op jit(solution)/shard_map/pallas_call | solution.py:89
  239.2 10.1 %all-reduce.3.cloned.1.call-done.h_ref = f32[256,512]{1,0:T(8,128)} async-done(((f32[256,512]{1,0:T(8,128)}), f32[256,512]{1,0:T(8,128)}) %all-reduce.3.cloned.1.call-update) | async-done | bytes 524304 | tf_op jit(solution)/shard_map/psum | solution.py:137
  249.3 0.0 copy-start.1
  249.3 1.0 copy-done.1
  250.3 2.9 %shard_map.47 = f32[256,512]{1,0:T(8,128)} custom-call(f32[256,512]{1,0:T(8,128)S(1)} %copy-done.1, f32[4,128,512]{2,1,0:T(8,128)S(1)} %get-tuple-element.7.u_ref, f32[4,128,128]{2,1,0:T(8,128)S(1)} %get-tuple-element.8.inv_ref), custom_call_target="tpu_custom_call" | custom-call | tf_op jit(solution)/shard_map/pallas_call | solution.py:108
Async XLA Ops:
  7.4 2.3 copy-start
  7.4 87.7 %reduce-scatter.2.cloned.1.call-start = ((), (), s32[]{:S(2)}) async-start(), calls=%async_computation.1 | async-start | bytes 4718592 | tf_op jit(solution)/shard_map/reduce_scatter | solution.py:136
  9.6 7.8 %copy-start.4 = (bf16[2048,2048]{1,0:T(8,128)(2,1)S(1)}, bf16[2048,2048]{1,0:T(8,128)(2,1)}, u32[]{:S(2)}) copy-start(bf16[2048,2048]{1,0:T(8,128)(2,1)} %param.4) | copy-start | bytes 25165828
  17.4 4.6 %copy-start.3 = (f32[2048,512]{1,0:T(8,128)}, f32[2048,512]{1,0:T(8,128)S(1)}, u32[]{:S(2)}) copy-start(f32[2048,512]{1,0:T(8,128)S(1)} %fusion.2) | copy-start | bytes 12582916
  43.7 158.4 %all-reduce.5.cloned.1.call-start = ((), (), s32[]{:S(2)}) async-start(), calls=%async_computation.3 | async-start | bytes 2097152 | tf_op jit(solution)/shard_map/psum | solution.py:133
  56.3 193.0 %all-reduce.3.cloned.1.call-start = ((), (), s32[]{:S(2)}) async-start(), calls=%async_computation.2 | async-start | bytes 1048576 | tf_op jit(solution)/shard_map/psum | solution.py:137
  202.1 1.2 copy-start.2
  249.3 1.0 copy-start.1
Sparse Core Ops, SparseCore 0:
  43.8 51.2 reduce-scatter.1
Sparse Core Ops, SparseCore 1:
  56.4 145.6 all-reduce.4
  205.2 44.0 all-reduce.2
where the time goes:
time: 263 us; the launch traced here: 261 us
  waiting for transfers between devices  156 us (59%)
  Pallas kernels  38.8 us (15%)
  matrix products  29.6 us (11%)
  local copies, waits for them, and re-layouts  15.3 us (6%)
  between operations  14.9 us (6%)
  other arithmetic  6.03 us (2%)
    psum x1, waiting for transfers between devices, body(): gram = lax.psum(local_gram, ('cohort', 'dev'))  107 us
    reduce_scatter x1, waiting for transfers between devices, body(): owned = lax.psum_scatter(product, 'dev', scatter_dimension=0, tiled=True)  38.7 us
    pallas_call x1, Pallas kernels, chol(): pl.pallas_call(chol_kernel, out_shape=(jax.ShapeDtypeStruct((nb, NB, k),...  35.9 us
    dot_general x4, matrix products, tdot(): lax.dot_general(a, b, (((0,), (0,)), ((), ())), preferred_element_type=jn...  21.8 us
    gather x1, local copies, waits for them, and re-layouts, body(): product = jnp.take(product, owner_perm, axis=0)  11.7 us
    psum x1, waiting for transfers between devices, body(): owned = lax.psum(owned, 'cohort')  10.1 us
    dot_general x1, matrix products, body(): sketch = jnp.dot(centered, probes, preferred_element_type=jnp.float32)  7.75 us
  transfers between devices with their start and end apart: 3, of which 3 were waited for; matrix products, arithmetic and copies ran while one was open for 5% of the time, Pallas kernels for 14%

commit v1 on v0

--- a/solution.py
+++ b/solution.py
@@ -38,13 +38,15 @@
             w_ref[base:, :] = w_ref[base:, :] - upd[base:, :]
 
 
-def cholesky_loop(a_ref, u_ref, inv_ref, w_ref):
+def cholesky_loop(a_ref, u_ref, inv_ref, w_ref, between=None):
     nb = a_ref.shape[0]
     eye = (
         lax.broadcasted_iota(jnp.int32, (NB, NB), 0) == lax.broadcasted_iota(jnp.int32, (NB, NB), 1)
     ).astype(jnp.float32)
 
     def step(b, c):
+        if between is not None:
+            pl.when(b == nb // 2)(between)
         at = pl.ds(pl.multiple_of(b * NB, NB), NB)
         w_ref[:, :NB] = a_ref[b, :, at]
         w_ref[:, NB:] = eye
@@ -76,49 +78,191 @@
     return jnp.concatenate(xs, axis=1)
 
 
-def chol_kernel(g_ref, u_ref, inv_ref, a_ref, w_ref):
-    nb = u_ref.shape[0]
+MESH = pl.DeviceIdType.MESH
+
+
+def kernel(shape, g_ref, h_ref, o_ref, gc, gacc, gq, gz, gzb, gout, hc, hacc, hq, hz, hzb, a_ref, u_ref, inv_ref, w_ref, send, recv):
+    groups, lanes_z = shape
+    coh, dev = lax.axis_index("cohort"), lax.axis_index("dev")
+    core, z = lax.rem(dev, 2), dev // 2
+    half, rq, rz = gc.shape[0], gq.shape[1], gzb.shape[1]
+
+    def at_cohort(k):
+        return lax.rem(coh + k, groups)
+
+    def at_z(k):
+        return lax.rem(z + k, lanes_z)
+
+    core_peer = (coh, 2 * z + 1 - core)
+    cohort_peers = [(at_cohort(k), dev) for k in range(1, groups)]
+    z_peers = [(coh, 2 * at_z(k) + core) for k in range(1, lanes_z)]
+    used = [0]
+
+    def copy(src, dst, peer):
+        n = used[0]
+        used[0] += 1
+        return pltpu.make_async_remote_copy(
+            src_ref=src, dst_ref=dst, send_sem=send.at[n], recv_sem=recv.at[n],
+            device_id=peer, device_id_type=MESH,
+        )
+
+    def start(copies):
+        for c in copies:
+            c.start()
+
+    def wait(copies):
+        for c in copies:
+            c.wait()
+
+    def rows(at, size):
+        return pl.ds(pl.multiple_of(at * size, 8), size)
+
+    barrier = pltpu.get_barrier_semaphore()
+    peers = [core_peer] + cohort_peers + z_peers
+    for peer in peers:
+        pl.semaphore_signal(barrier, inc=1, device_id=peer, device_id_type=MESH)
+    pl.semaphore_wait(barrier, len(peers))
+
+    g1 = [copy(g_ref.at[rows(1 - core, half)], gc, core_peer)]
+    h1 = [copy(h_ref.at[:, 1 - core], hc, core_peer)]
+    start(g1)
+    start(h1)
+    wait(g1)
+    gacc[...] = g_ref[rows(core, half), :] + gc[...]
+    g2 = [copy(gacc.at[rows(at_cohort(k), rq)], gq.at[k - 1], cohort_peers[k - 1]) for k in range(1, groups)]
+    start(g2)
+    wait(g2)
+    total = gacc[rows(coh, rq), :]
+    for k in range(groups - 1):
+        total = total + gq[k]
+    gz[...] = total
+    g3 = [copy(gz.at[rows(at_z(k), rz)], gzb.at[k - 1], z_peers[k - 1]) for k in range(1, lanes_z)]
+    start(g3)
+
+    wait(h1)
+
+    def add_core(i, c):
+        for q in range(groups):
+            hacc[q, i] = h_ref[i, core, q] + hc[i, q]
+        return c
+
+    lax.fori_loop(0, lanes_z, add_core, 0)
+
+    wait(g3)
+    total = gz[rows(z, rz), :]
+    for k in range(lanes_z - 1):
+        total = total + gzb[k]
+    own_q = core * groups + coh
+    own = rows(own_q * lanes_z + z, rz)
+    gout[own, :] = total
+    g4 = [copy(gout.at[own], gout.at[own], peer) for peer in z_peers]
+    start(g4)
+    wait(g4)
+    own = rows(own_q, rq)
+    g5 = [copy(gout.at[own], gout.at[own], peer) for peer in cohort_peers]
+    start(g5)
+    h2 = [copy(hacc.at[at_cohort(k)], hq.at[k - 1], cohort_peers[k - 1]) for k in range(1, groups)]
+    start(h2)
+    wait(g5)
+    own = rows(core, half)
+    g6 = [copy(gout.at[own], gout.at[own], core_peer)]
+    start(g6)
+    wait(g6)
+
+    nb = a_ref.shape[0]
+    n = 0
     for b in range(nb):
-        a_ref[b] = g_ref[b * NB : (b + 1) * NB, :]
-    cholesky_loop(a_ref, u_ref, inv_ref, w_ref)
-
-
-def chol(gram):
+        for c in range(nb):
+            cols = slice(c * NB, (c + 1) * NB)
+            if c < b:
+                a_ref[b, :, cols] = jnp.zeros((NB, NB), jnp.float32)
+            else:
+                a_ref[b, :, cols] = gout[n * NB : (n + 1) * NB, :]
+                n += 1
+
+    h3 = [copy(hz.at[at_z(k)], hzb.at[k - 1], z_peers[k - 1]) for k in range(1, lanes_z)]
+
+    def between():
+        wait(h2)
+
+        def add_cohort(i, c):
+            t = hacc[coh, i]
+            for k in range(groups - 1):
+                t = t + hq[k, i]
+            hz[i] = t
+            return c
+
+        lax.fori_loop(0, lanes_z, add_cohort, 0)
+        start(h3)
+
+    cholesky_loop(a_ref, u_ref, inv_ref, w_ref, between)
+    wait(h3)
+    h = hz[z]
+    for k in range(lanes_z - 1):
+        h = h + hzb[k]
+    rc = h.shape[0]
+    own = rows(coh, rc)
+    o_ref[own, :] = apply(h, u_ref, inv_ref)
+    h4 = [copy(o_ref.at[own], o_ref.at[own], peer) for peer in cohort_peers]
+    start(h4)
+    wait(h4)
+
+
+def reduce_and_apply(gram, product, groups, devs):
     k = gram.shape[0]
     nb = k // NB
+    m = product.shape[0]
+    z = devs // 2
+    r = m // devs
+    rc = r // groups
+    blocks = [gram[b * NB : (b + 1) * NB, c * NB : (c + 1) * NB] for b in range(nb) for c in range(b, nb)]
+    count = len(blocks) * NB
+    unit = 8 * groups * devs
+    total = -(-count // unit) * unit
+    if total > count:
+        blocks.append(jnp.zeros((total - count, NB), jnp.float32))
+    packed = jnp.concatenate(blocks, axis=0)
+    product = product.reshape(z, 2, groups, rc, k)
+    half = total // 2
+    rq = half // groups
+    rz = rq // z
+    copies = 3 + 4 * (groups - 1) + 3 * (z - 1)
+    f32 = jnp.float32
     return pl.pallas_call(
-        chol_kernel,
-        out_shape=(
-            jax.ShapeDtypeStruct((nb, NB, k), jnp.float32),
-            jax.ShapeDtypeStruct((nb, NB, NB), jnp.float32),
+        lambda *refs: kernel((groups, z), *refs),
+        out_shape=jax.ShapeDtypeStruct((r, k), f32),
+        in_specs=[pl.BlockSpec(memory_space=pltpu.VMEM)] * 2,
+        out_specs=pl.BlockSpec(memory_space=pltpu.VMEM),
+        scratch_shapes=[
+            pltpu.VMEM((half, NB), f32),
+            pltpu.VMEM((half, NB), f32),
+            pltpu.VMEM((groups - 1, rq, NB), f32),
+            pltpu.VMEM((rq, NB), f32),
+            pltpu.VMEM((z - 1, rz, NB), f32),
+            pltpu.VMEM((total, NB), f32),
+            pltpu.VMEM((z, groups, rc, k), f32),
+            pltpu.VMEM((groups, z, rc, k), f32),
+            pltpu.VMEM((groups - 1, z, rc, k), f32),
+            pltpu.VMEM((z, rc, k), f32),
+            pltpu.VMEM((z - 1, rc, k), f32),
+            pltpu.VMEM((nb, NB, k), f32),
+            pltpu.VMEM((nb, NB, k), f32),
+            pltpu.VMEM((nb, NB, NB), f32),
+            pltpu.VMEM((NB, 2 * NB), f32),
+            pltpu.SemaphoreType.DMA((copies,)),
+            pltpu.SemaphoreType.DMA((copies,)),
+        ],
+        compiler_params=pltpu.CompilerParams(
+            vmem_limit_bytes=40 << 20, collective_id=0, has_side_effects=True
         ),
-        in_specs=[pl.BlockSpec(memory_space=pltpu.VMEM)],
-        out_specs=(pl.BlockSpec(memory_space=pltpu.VMEM),) * 2,
-        scratch_shapes=[pltpu.VMEM((nb, NB, k), jnp.float32), pltpu.VMEM((NB, 2 * NB), jnp.float32)],
-        compiler_params=pltpu.CompilerParams(vmem_limit_bytes=32 << 20),
-        cost_estimate=pl.CostEstimate(flops=10**10, bytes_accessed=4 << 20, transcendentals=0),
-    )(gram)
-
-
-def apply_kernel(h_ref, u_ref, inv_ref, o_ref):
-    o_ref[...] = apply(h_ref[...], u_ref, inv_ref)
-
-
-def apply_inv(h, u, inv):
-    return pl.pallas_call(
-        apply_kernel,
-        out_shape=jax.ShapeDtypeStruct(h.shape, jnp.float32),
-        in_specs=[pl.BlockSpec(memory_space=pltpu.VMEM)] * 3,
-        out_specs=pl.BlockSpec(memory_space=pltpu.VMEM),
-        compiler_params=pltpu.CompilerParams(vmem_limit_bytes=32 << 20),
-    )(h, u, inv)
+    )(packed, product)
 
 
 def tdot(a, b):
     return lax.dot_general(a, b, (((0,), (0,)), ((), ())), preferred_element_type=jnp.float32)
 
 
-def body(dosage, allele_freq, probes, owner_perm):
+def body(groups, devs, dosage, allele_freq, probes, owner_perm):
     mean_dose = 2.0 * allele_freq
     inv_spread = 1.0 / jnp.sqrt(2.0 * allele_freq * (1.0 - allele_freq))
     centered = ((dosage.astype(jnp.float32) - mean_dose[None, :]) * inv_spread[None, :]).astype(
@@ -130,18 +274,14 @@
     low = (sketch - rounded).astype(jnp.bfloat16)
     cross = tdot(high, low)
     local_gram = tdot(high, high) + (cross + cross.T)
-    gram = lax.psum(local_gram, ("cohort", "dev"))
     product = tdot(centered, high) + tdot(centered, low)
     product = jnp.take(product, owner_perm, axis=0)
-    owned = lax.psum_scatter(product, "dev", scatter_dimension=0, tiled=True)
-    owned = lax.psum(owned, "cohort")
-    u, inv = chol(gram)
-    return apply_inv(owned, u, inv)
+    return reduce_and_apply(local_gram, product, groups, devs)
 
 
 def solution(mesh):
     return jax.shard_map(
-        body,
+        lambda *args: body(mesh.shape["cohort"], mesh.shape["dev"], *args),
         mesh=mesh,
         in_specs=(P(("cohort", "dev"), None), P(), P(), P()),
         out_specs=P("dev", None),

time: 263 us -> 131 us (0.50)
  waiting for transfers between devices: 156 us -> 0 us
  Pallas kernels: 38.8 us -> 79.8 us
  between operations: 14.9 us -> 0.18 us
  other arithmetic: 6.03 us -> 3.33 us
  local copies, waits for them, and re-layouts: 15.3 us -> 18 us
    psum x2 -> x0, waiting for transfers between devices: 117 us -> none  [the longest x1 107 us: body(): gram = lax.psum(local_gram, ('cohort', 'dev'))]
    pallas_call x2 -> x1, Pallas kernels: 38.8 us -> 79.8 us  [reduce_and_apply(): pl.pallas_call(lambda *refs: kernel((groups, z), *refs), out_shape=jax.Sh...]
    reduce_scatter x1 -> x0, waiting for transfers between devices: 38.7 us -> none  [body(): owned = lax.psum_scatter(product, 'dev', scatter_dimension=0, tiled=True)]
  transfers between devices with their start and end apart: 3 -> 0, of which waited for: 3 -> 0; matrix products, arithmetic and copies ran while one was open for 5% -> 0% of each run, Pallas kernels for 14% -> 0%
where the time goes in v1:
time: 131 us; the launch traced here: 129 us
  Pallas kernels  79.8 us (61%)
  matrix products  27.8 us (21%)
  local copies, waits for them, and re-layouts  18 us (14%)
  other arithmetic  3.33 us (3%)
    pallas_call x1, Pallas kernels, reduce_and_apply(): pl.pallas_call(lambda *refs: kernel((groups, z), *refs), out_shape=jax.Sh...  79.8 us
    dot_general x4, matrix products, tdot(): lax.dot_general(a, b, (((0,), (0,)), ((), ())), preferred_element_type=jn...  20.9 us
    gather x1, local copies, waits for them, and re-layouts, body(): product = jnp.take(product, owner_perm, axis=0)  11.8 us
    dot_general x1, matrix products, body(): sketch = jnp.dot(centered, probes, preferred_element_type=jnp.float32)  6.88 us
    unnamed x21, local copies, waits for them, and re-layouts  3.59 us

profile of v1, /device:TPU:14, one launch (start us, length us, event | category | flops | bytes accessed | tf_op | source)
XLA Modules:
  0.0 129.1 jit_solution(2442058955458126930)
XLA Ops:
  0.0 0.0 copy-start
  0.0 0.9 broadcast_multiply_fusion
  0.9 0.8 copy-done
  1.6 6.9 %fusion.2 = f32[2048,512]{1,0:T(8,128)S(1)} fusion(bf16[2048,512]{1,0:T(8,128)(2,1)S(1)} %copy-done, bf16[2048,2048]{1,0:T(8,128)(2,1)} %param.4, f32[2048]{0:T(1024)S(1)} %get-tuple-element.6, f32[2048]{0:T(1024)S(1)} %get-tuple-element.5), kind=kOutput, calls=%fused_computation.6 | convolution fusion | flops 4311744512 | bytes 14696448 | tf_op jit(solution)/shard_map/dot_general | solution.py:271
  8.5 0.0 copy-start.1
  8.5 1.9 %copy-done.1 = f32[2048,512]{1,0:T(8,128)} copy-done((f32[2048,512]{1,0:T(8,128)}, f32[2048,512]{1,0:T(8,128)S(1)}, u32[]{:S(2)}) %copy-start.1) | copy-done | bytes 4194328
  10.4 2.2 %fusion.6 = f32[512,512]{1,0:T(8,128)} fusion(f32[2048,512]{1,0:T(8,128)S(1)} %fusion.2), kind=kOutput, calls=%fused_computation.12 | convolution fusion | flops 1078984704 | bytes 5242880 | tf_op jit(solution)/shard_map/dot_general | solution.py:262
  12.7 2.6 %copy.5 = f32[512,512]{0,1:T(8,128)} copy(f32[512,512]{1,0:T(8,128)} %fusion.6) | data formatting | bytes 2097152 | tf_op jit(solution)/shard_map/dot_general | solution.py:262
  15.2 0.0 copy-start.2
  15.3 5.4 %convolution_add_fusion = f32[512,512]{1,0:T(8,128)S(1)} fusion(f32[512,512]{1,0:T(8,128)} %fusion.6, f32[512,512]{0,1:T(8,128)} %copy.5, f32[2048,512]{1,0:T(8,128)} %copy-done.1), kind=kOutput, calls=%fused_computation.10 | convolution fusion | flops 1076363264 | bytes 7340032 | tf_op jit(solution)/shard_map/dot_general | solution.py:262
  20.7 0.0 slice-start
  20.9 0.0 copy-done.2
  20.9 0.0 slice-start.1
  20.9 7.1 %fusion = f32[2048,512]{1,0:T(8,128)S(1)} fusion(bf16[2048,2048]{1,0:T(8,128)(2,1)} %param.4, f32[2048]{0:T(1024)S(1)} %get-tuple-element.6, f32[2048]{0:T(1024)S(1)} %get-tuple-element.5, f32[2048,512]{1,0:T(8,128)S(1)} %copy-done.2), kind=kOutput, calls=%fused_computation.4 | convolution fusion | flops 4314890240 | bytes 16793600 | tf_op jit(solution)/shard_map/dot_general | solution.py:262
  28.0 0.0 slice-done
  28.0 0.0 slice-done.1
  28.1 0.0 copy-start.3
  28.1 6.1 %fusion.4 = f32[2048,512]{1,0:T(8,128)} fusion(f32[2048,512]{1,0:T(8,128)S(1)} %fusion, bf16[2048,2048]{1,0:T(8,128)(2,1)S(1)} %bitcast.8, f32[2048]{0:T(1024)S(1)} %get-tuple-element.6, f32[2048]{0:T(1024)S(1)} %get-tuple-element.5, f32[2048,512]{1,0:T(8,128)S(1)} %copy-done.2), kind=kOutput, calls=%fused_computation.8 | convolution fusion | flops 4314890240 | bytes 20987904 | tf_op jit(solution)/shard_map/dot_general | solution.py:262
  34.1 0.0 copy-done.3
  34.2 11.8 %gather_fusion = f32[2048,512]{1,0:T(8,128)} fusion(f32[2048,512]{1,0:T(8,128)} %fusion.4, s32[2048]{0:T(1024)S(1)} %fusion.8), kind=kCustom, calls=%fused_computation | custom fusion | bytes 8396800 | tf_op jit(solution)/shard_map/jit(_take)/gather | solution.py:278
  45.9 0.1 broadcast_in_dim.16
  46.0 2.5 %broadcast_select_fusion.refs_1_ = f32[4,2,4,64,512]{4,3,2,1,0:T(8,128)S(1)} fusion(f32[4,2,4,64,512]{4,3,2,1,0:T(8,128)} %bitcast.6, pred[4,2,4,64]{3,2,1,0:T(4,128)(4,1)S(1)} %broadcast_in_dim.16), kind=kLoop, calls=%fused_computation.9 | loop fusion | flops 1048576 | bytes 8390656 | tf_op jit(solution)/shard_map/jit(_take)/select_n | solution.py:278
  48.5 79.8 %shard_map.46 = f32[256,512]{1,0:T(8,128)S(1)} custom-call(f32[1280,128]{1,0:T(8,128)S(1)} %slice_dynamic-update-slice_fusion.refs_0_, f32[4,2,4,64,512]{4,3,2,1,0:T(8,128)S(1)} %broadcast_select_fusion.refs_1_), custom_call_target="tpu_custom_call" | custom-call | tf_op jit(solution)/shard_map/pallas_call | solution.py:231
  128.3 0.8 copy.15
  (12 shorter events, 0.1 us)
Async XLA Ops:
  0.0 1.6 %copy-start = (bf16[2048,512]{1,0:T(8,128)(2,1)S(1)}, bf16[2048,512]{1,0:T(8,128)(2,1)}, u32[]{:S(2)}) copy-start(bf16[2048,512]{1,0:T(8,128)(2,1)} %param.6) | copy-start | bytes 6291460
  8.5 1.9 %copy-start.1 = (f32[2048,512]{1,0:T(8,128)}, f32[2048,512]{1,0:T(8,128)S(1)}, u32[]{:S(2)}) copy-start(f32[2048,512]{1,0:T(8,128)S(1)} %fusion.2) | copy-start | bytes 12582916
  15.2 5.6 %copy-start.2 = (f32[2048,512]{1,0:T(8,128)S(1)}, f32[2048,512]{1,0:T(8,128)}, u32[]{:S(2)}) copy-start(f32[2048,512]{1,0:T(8,128)} %copy-done.1) | copy-start | bytes 12582916
  20.7 7.3 %slice-start = ((s8[8388608]{0:T(1024)(128)(4,1)}), s8[4194304]{0:T(1024)(128)(4,1)S(1)}, s32[]{:S(2)}) async-start(s8[8388608]{0:T(1024)(128)(4,1)} %bitcast.7), calls=%async_computation | async-start | bytes 8388608
  20.9 7.2 %slice-start.1 = ((s8[8388608]{0:T(1024)(128)(4,1)}), s8[4194304]{0:T(1024)(128)(4,1)S(1)}, s32[]{:S(2)}) async-start(s8[8388608]{0:T(1024)(128)(4,1)} %bitcast.7), calls=%async_computation.1 | async-start | bytes 8388608
  28.1 6.1 %copy-start.3 = (s32[2048]{0:T(1024)S(1)}, s32[2048]{0:T(1024)}, u32[]{:S(2)}) copy-start(s32[2048]{0:T(1024)} %param.7) | copy-start | bytes 24580

commit v2 on v1

--- a/solution.py
+++ b/solution.py
@@ -45,8 +45,8 @@
     ).astype(jnp.float32)
 
     def step(b, c):
-        if between is not None:
-            pl.when(b == nb // 2)(between)
+        for at_block, act in (between or {}).items():
+            pl.when(b == at_block)(act)
         at = pl.ds(pl.multiple_of(b * NB, NB), NB)
         w_ref[:, :NB] = a_ref[b, :, at]
         w_ref[:, NB:] = eye
@@ -81,7 +81,7 @@
 MESH = pl.DeviceIdType.MESH
 
 
-def kernel(shape, g_ref, h_ref, o_ref, gc, gacc, gq, gz, gzb, gout, hc, hacc, hq, hz, hzb, a_ref, u_ref, inv_ref, w_ref, send, recv):
+def kernel(shape, perm_ref, g_ref, c_hbm, s_hbm, o_ref, c_ref, s_ref, hv, h_ref, local, gc, gacc, gq, gz, gzb, gout, hc, hacc, hq, hz, hzb, a_ref, u_ref, inv_ref, w_ref, send, recv):
     groups, lanes_z = shape
     coh, dev = lax.axis_index("cohort"), lax.axis_index("dev")
     core, z = lax.rem(dev, 2), dev // 2
@@ -117,6 +117,26 @@
     def rows(at, size):
         return pl.ds(pl.multiple_of(at * size, 8), size)
 
+    loads = [
+        pltpu.make_async_copy(c_hbm, c_ref, local.at[0]),
+        pltpu.make_async_copy(s_hbm, s_ref, local.at[1]),
+    ]
+    start(loads)
+    chunk = NB * 2
+    count = c_ref.shape[1] // chunk
+    k_cols = o_ref.shape[1]
+
+    def multiply(first, last):
+        def one(i, c):
+            at = pl.ds(pl.multiple_of(i * chunk, chunk), chunk)
+            both = lax.dot_general(
+                c_ref[:, at], s_ref[...], (((0,), (0,)), ((), ())), preferred_element_type=jnp.float32
+            )
+            hv[at, :] = both[:, :k_cols] + both[:, k_cols:]
+            return c
+
+        lax.fori_loop(first, last, one, 0)
+
     barrier = pltpu.get_barrier_semaphore()
     peers = [core_peer] + cohort_peers + z_peers
     for peer in peers:
@@ -126,11 +146,13 @@
     g1 = [copy(g_ref.at[rows(1 - core, half)], gc, core_peer)]
     h1 = [copy(h_ref.at[:, 1 - core], hc, core_peer)]
     start(g1)
-    start(h1)
+    wait(loads)
+    multiply(0, count // 8)
     wait(g1)
     gacc[...] = g_ref[rows(core, half), :] + gc[...]
     g2 = [copy(gacc.at[rows(at_cohort(k), rq)], gq.at[k - 1], cohort_peers[k - 1]) for k in range(1, groups)]
     start(g2)
+    multiply(count // 8, 3 * count // 8)
     wait(g2)
     total = gacc[rows(coh, rq), :]
     for k in range(groups - 1):
@@ -139,15 +161,7 @@
     g3 = [copy(gz.at[rows(at_z(k), rz)], gzb.at[k - 1], z_peers[k - 1]) for k in range(1, lanes_z)]
     start(g3)
 
-    wait(h1)
-
-    def add_core(i, c):
-        for q in range(groups):
-            hacc[q, i] = h_ref[i, core, q] + hc[i, q]
-        return c
-
-    lax.fori_loop(0, lanes_z, add_core, 0)
-
+    multiply(3 * count // 8, count // 2)
     wait(g3)
     total = gz[rows(z, rz), :]
     for k in range(lanes_z - 1):
@@ -157,17 +171,36 @@
     gout[own, :] = total
     g4 = [copy(gout.at[own], gout.at[own], peer) for peer in z_peers]
     start(g4)
+    multiply(count // 2, 5 * count // 8)
     wait(g4)
     own = rows(own_q, rq)
     g5 = [copy(gout.at[own], gout.at[own], peer) for peer in cohort_peers]
     start(g5)
-    h2 = [copy(hacc.at[at_cohort(k)], hq.at[k - 1], cohort_peers[k - 1]) for k in range(1, groups)]
-    start(h2)
+    multiply(5 * count // 8, count)
     wait(g5)
     own = rows(core, half)
     g6 = [copy(gout.at[own], gout.at[own], core_peer)]
     start(g6)
+
+    rc = h_ref.shape[3]
+
+    def owner(i, c):
+        iz, i1 = i // (2 * groups), lax.rem(i, 2 * groups)
+        ic, iq = i1 // groups, lax.rem(i1, groups)
+
+        def eight(j, c):
+            for t in range(8):
+                row = perm_ref[i * rc + j * 8 + t]
+                h_ref[iz, ic, iq, pl.ds(j * 8 + t, 1), :] = hv[pl.ds(row, 1), :]
+            return c
+
+        lax.fori_loop(0, rc // 8, eight, 0)
+        return c
+
+    lax.fori_loop(0, lanes_z * 2 * groups, owner, 0)
+    start(h1)
     wait(g6)
+    h2 = [copy(hacc.at[at_cohort(k)], hq.at[k - 1], cohort_peers[k - 1]) for k in range(1, groups)]
 
     nb = a_ref.shape[0]
     n = 0
@@ -182,7 +215,18 @@
 
     h3 = [copy(hz.at[at_z(k)], hzb.at[k - 1], z_peers[k - 1]) for k in range(1, lanes_z)]
 
-    def between():
+    def first():
+        wait(h1)
+
+        def add_core(i, c):
+            for q in range(groups):
+                hacc[q, i] = h_ref[i, core, q] + hc[i, q]
+            return c
+
+        lax.fori_loop(0, lanes_z, add_core, 0)
+        start(h2)
+
+    def second():
         wait(h2)
 
         def add_cohort(i, c):
@@ -195,12 +239,11 @@
         lax.fori_loop(0, lanes_z, add_cohort, 0)
         start(h3)
 
-    cholesky_loop(a_ref, u_ref, inv_ref, w_ref, between)
+    cholesky_loop(a_ref, u_ref, inv_ref, w_ref, {1: first, nb - 1: second})
     wait(h3)
     h = hz[z]
     for k in range(lanes_z - 1):
         h = h + hzb[k]
-    rc = h.shape[0]
     own = rows(coh, rc)
     o_ref[own, :] = apply(h, u_ref, inv_ref)
     h4 = [copy(o_ref.at[own], o_ref.at[own], peer) for peer in cohort_peers]
@@ -208,10 +251,10 @@
     wait(h4)
 
 
-def reduce_and_apply(gram, product, groups, devs):
+def reduce_and_apply(gram, centered, parts, owner_perm, groups, devs):
     k = gram.shape[0]
     nb = k // NB
-    m = product.shape[0]
+    m = centered.shape[1]
     z = devs // 2
     r = m // devs
     rc = r // groups
@@ -222,7 +265,6 @@
     if total > count:
         blocks.append(jnp.zeros((total - count, NB), jnp.float32))
     packed = jnp.concatenate(blocks, axis=0)
-    product = product.reshape(z, 2, groups, rc, k)
     half = total // 2
     rq = half // groups
     rz = rq // z
@@ -231,9 +273,19 @@
     return pl.pallas_call(
         lambda *refs: kernel((groups, z), *refs),
         out_shape=jax.ShapeDtypeStruct((r, k), f32),
-        in_specs=[pl.BlockSpec(memory_space=pltpu.VMEM)] * 2,
+        in_specs=[
+            pl.BlockSpec(memory_space=pltpu.SMEM),
+            pl.BlockSpec(memory_space=pltpu.VMEM),
+            pl.BlockSpec(memory_space=pl.ANY),
+            pl.BlockSpec(memory_space=pl.ANY),
+        ],
         out_specs=pl.BlockSpec(memory_space=pltpu.VMEM),
         scratch_shapes=[
+            pltpu.VMEM(centered.shape, centered.dtype),
+            pltpu.VMEM(parts.shape, parts.dtype),
+            pltpu.VMEM((m, k), f32),
+            pltpu.VMEM((z, 2, groups, rc, k), f32),
+            pltpu.SemaphoreType.DMA((2,)),
             pltpu.VMEM((half, NB), f32),
             pltpu.VMEM((half, NB), f32),
             pltpu.VMEM((groups - 1, rq, NB), f32),
@@ -253,9 +305,9 @@
             pltpu.SemaphoreType.DMA((copies,)),
         ],
         compiler_params=pltpu.CompilerParams(
-            vmem_limit_bytes=40 << 20, collective_id=0, has_side_effects=True
+            vmem_limit_bytes=56 << 20, collective_id=0, has_side_effects=True
         ),
-    )(packed, product)
+    )(owner_perm, packed, centered, parts)
 
 
 def tdot(a, b):
@@ -272,11 +324,9 @@
     rounded = lax.reduce_precision(sketch, 8, 7)
     high = rounded.astype(jnp.bfloat16)
     low = (sketch - rounded).astype(jnp.bfloat16)
-    cross = tdot(high, low)
-    local_gram = tdot(high, high) + (cross + cross.T)
-    product = tdot(centered, high) + tdot(centered, low)
-    product = jnp.take(product, owner_perm, axis=0)
-    return reduce_and_apply(local_gram, product, groups, devs)
+    local_gram = tdot(high, high) + (tdot(high, low) + tdot(low, high))
+    parts = jnp.concatenate([high, low], axis=1)
+    return reduce_and_apply(local_gram, centered, parts, owner_perm, groups, devs)
 
 
 def solution(mesh):

time: 131 us -> 118 us (0.901); the launches traced: 129 us -> 118 us
  local copies, waits for them, and re-layouts: 18 us -> 1.98 us
  matrix products: 27.8 us -> 12 us
  Pallas kernels: 79.8 us -> 90.1 us
  other arithmetic: 3.33 us -> 13.3 us
    dot_general x4 -> x3, matrix products: 20.9 us -> 3.83 us  [tdot(): lax.dot_general(a, b, (((0,), (0,)), ((), ())), preferred_element_type=jn...]
    gather x1 -> x0, local copies, waits for them, and re-layouts: 11.8 us -> none  [body(): product = jnp.take(product, owner_perm, axis=0)]
    pallas_call x1, Pallas kernels: 79.8 us -> 90.1 us  [reduce_and_apply(): pl.pallas_call(lambda *refs: kernel((groups, z), *refs), out_shape=jax.Sh...]
    convert_element_type x0 -> x1, other arithmetic: none -> 9.81 us  [body(): ((dosage.astype(jnp.float32) - mean_dose[None, :]) * inv_spread[None, :])...]
    concatenate x0 -> x1, other arithmetic: none -> 2.61 us  [body(): parts = jnp.concatenate([high, low], axis=1)]
    dot_general x1 -> x0, local copies, waits for them, and re-layouts: 2.57 us -> none  [tdot(): lax.dot_general(a, b, (((0,), (0,)), ((), ())), preferred_element_type=jn...]
    select_n x1 -> x0, other arithmetic: 2.46 us -> none  [body(): product = jnp.take(product, owner_perm, axis=0)]
    unnamed x21 -> x13, local copies, waits for them, and re-layouts: 3.59 us -> 1.97 us
where the time goes in v2:
time: 118 us
  Pallas kernels  90.1 us (76%)
  other arithmetic  13.3 us (11%)
  matrix products  12 us (10%)
  local copies, waits for them, and re-layouts  1.98 us (2%)
    pallas_call x1, Pallas kernels, reduce_and_apply(): pl.pallas_call(lambda *refs: kernel((groups, z), *refs), out_shape=jax.Sh...  90.1 us
    convert_element_type x1, other arithmetic, body(): ((dosage.astype(jnp.float32) - mean_dose[None, :]) * inv_spread[None, :])...  9.81 us
    dot_general x1, matrix products, body(): sketch = jnp.dot(centered, probes, preferred_element_type=jnp.float32)  8.21 us
    dot_general x3, matrix products, tdot(): lax.dot_general(a, b, (((0,), (0,)), ((), ())), preferred_element_type=jn...  3.83 us
    concatenate x1, other arithmetic, body(): parts = jnp.concatenate([high, low], axis=1)  2.61 us

profile of v2, /device:TPU:14, one launch (start us, length us, event | category | flops | bytes accessed | tf_op | source)
XLA Modules:
  0.0 117.5 jit_solution(14707519816817481451)
XLA Ops:
  0.0 0.0 copy-start
  0.0 0.9 broadcast_multiply_fusion
  0.9 9.8 %multiply_convert_fusion.refs_2_ = bf16[2048,2048]{1,0:T(8,128)(2,1)} fusion(bf16[2048,2048]{1,0:T(8,128)(2,1)} %param.4, f32[2048]{0:T(1024)S(1)} %get-tuple-element.8, f32[2048]{0:T(1024)S(1)} %get-tuple-element.7), kind=kLoop, calls=%fused_computation | loop fusion | flops 16777216 | bytes 16793600 | tf_op jit(solution)/shard_map/convert_element_type | solution.py:320
  10.7 0.0 copy-done
  10.7 8.2 %fusion = (bf16[2048,512]{1,0:T(8,128)(2,1)S(1)}, bf16[2048,512]{1,0:T(8,128)(2,1)S(1)}) fusion(bf16[2048,2048]{1,0:T(8,128)(2,1)} %multiply_convert_fusion.refs_2_, bf16[2048,512]{1,0:T(8,128)(2,1)S(1)} %copy-done), kind=kOutput, calls=%fused_computation.3 | convolution fusion | flops 4299161600 | bytes 14680064 | tf_op jit(solution)/shard_map/dot_general | solution.py:323
  18.9 1.3 %fusion.3 = f32[512,512]{1,0:T(8,128)S(1)} fusion(bf16[2048,512]{1,0:T(8,128)(2,1)S(1)} %get-tuple-element.6, bf16[2048,512]{1,0:T(8,128)(2,1)S(1)} %get-tuple-element.5), kind=kOutput, calls=%fused_computation.19 | convolution fusion | flops 1073741824 | bytes 5242880 | tf_op jit(solution)/shard_map/dot_general | solution.py:314
  20.2 1.3 %fusion.2 = f32[512,512]{1,0:T(8,128)S(1)} fusion(bf16[2048,512]{1,0:T(8,128)(2,1)S(1)} %get-tuple-element.6), kind=kOutput, calls=%fused_computation.18 | convolution fusion | flops 1073741824 | bytes 3145728 | tf_op jit(solution)/shard_map/dot_general | solution.py:314
  21.4 1.3 %fusion.1 = f32[512,512]{1,0:T(8,128)S(1)} fusion(f32[512,512]{1,0:T(8,128)S(1)} %fusion.2, f32[512,512]{1,0:T(8,128)S(1)} %fusion.3, bf16[2048,512]{1,0:T(8,128)(2,1)S(1)} %get-tuple-element.5, bf16[2048,512]{1,0:T(8,128)(2,1)S(1)} %get-tuple-element.6), kind=kOutput, calls=%fused_computation.6 | convolution fusion | flops 1074266112 | bytes 7340032 | tf_op jit(solution)/shard_map/dot_general | solution.py:314
  22.9 0.0 copy-start.1
  22.9 2.6 %pad_maximum_fusion.refs_3_ = bf16[2048,1024]{1,0:T(8,128)(2,1)} fusion(bf16[2048,512]{1,0:T(8,128)(2,1)S(1)} %get-tuple-element.5, bf16[2048,512]{1,0:T(8,128)(2,1)S(1)} %get-tuple-element.6), kind=kLoop, calls=%fused_computation.4 | loop fusion | flops 8388608 | bytes 8388608 | tf_op jit(solution)/shard_map/concatenate | solution.py:328
  25.5 0.0 copy-done.1
  25.5 90.1 %shard_map.46 = f32[256,512]{1,0:T(8,128)} custom-call(s32[2048]{0:T(1024)} %refs_0_.1, f32[1280,128]{1,0:T(8,128)} %copy-done.1, bf16[2048,2048]{1,0:T(8,128)(2,1)} %multiply_convert_fusion.refs_2_, bf16[2048,1024]{1,0:T(8,128)(2,1)} %pad_maximum_fusion.refs_3_), custom_call_target="tpu_custom_call" | custom-call | tf_op jit(solution)/shard_map/pallas_call | solution.py:273
  115.6 1.9 %copy.17 = f32[256,512]{1,0:T(8,128)} copy(f32[256,512]{1,0:T(8,128)} %shard_map.46) | data formatting | bytes 1048576
  (9 shorter events, 0.1 us)
Async XLA Ops:
  0.0 10.7 %copy-start = (bf16[2048,512]{1,0:T(8,128)(2,1)S(1)}, bf16[2048,512]{1,0:T(8,128)(2,1)}, u32[]{:S(2)}) copy-start(bf16[2048,512]{1,0:T(8,128)(2,1)} %param.6) | copy-start | bytes 6291460
  22.9 2.6 %copy-start.1 = (f32[1280,128]{1,0:T(8,128)}, f32[1280,128]{1,0:T(8,128)S(1)}, u32[]{:S(2)}) copy-start(f32[1280,128]{1,0:T(8,128)S(1)} %slice_dynamic-update-slice_fusion.refs_1_) | copy-start | bytes 1966084

commit v3 on v2

--- a/solution.py
+++ b/solution.py
@@ -13,6 +13,20 @@
     return lax.dot_general(
         a, b, (((ca,), (cb,)), ((), ())), precision=HI, preferred_element_type=jnp.float32
     )
+
+
+def split(x):
+    high = x.astype(jnp.bfloat16).astype(jnp.float32)
+    mid = (x - high).astype(jnp.bfloat16).astype(jnp.float32)
+    return high, mid, x - high - mid
+
+
+def dot_parts(a, b):
+    ah, am, al = split(a)
+    bh, bm, bl = split(b)
+    left = jnp.concatenate([ah, ah, am, ah, am, al], axis=0).astype(jnp.bfloat16)
+    right = jnp.concatenate([bh, bm, bh, bl, bm, bh], axis=0).astype(jnp.bfloat16)
+    return lax.dot_general(left, right, (((0,), (0,)), ((), ())), preferred_element_type=jnp.float32)
 
 
 def factor_block(w_ref):
@@ -34,7 +48,7 @@
         if lo + 8 < NB:
             base = (lo + 8) // 8 * 8
             left = panel[:, :NB]
-            upd = dot(left, panel, 0, 0)
+            upd = dot_parts(left, panel)
             w_ref[base:, :] = w_ref[base:, :] - upd[base:, :]
 
 

time: 118 us -> 114 us (0.966)
  Pallas kernels: 90.1 us -> 86.3 us
    pallas_call x1, Pallas kernels: 90.1 us -> 86.3 us  [reduce_and_apply(): pl.pallas_call(lambda *refs: kernel((groups, z), *refs), out_shape=jax.Sh...]
where the time goes in v3:
time: 114 us
  Pallas kernels  86.3 us (76%)
  other arithmetic  13.3 us (12%)
  matrix products  12 us (11%)
  local copies, waits for them, and re-layouts  1.98 us (2%)
    pallas_call x1, Pallas kernels, reduce_and_apply(): pl.pallas_call(lambda *refs: kernel((groups, z), *refs), out_shape=jax.Sh...  86.3 us
    convert_element_type x1, other arithmetic, body(): ((dosage.astype(jnp.float32) - mean_dose[None, :]) * inv_spread[None, :])...  9.81 us
    dot_general x1, matrix products, body(): sketch = jnp.dot(centered, probes, preferred_element_type=jnp.float32)  8.21 us
    dot_general x3, matrix products, tdot(): lax.dot_general(a, b, (((0,), (0,)), ((), ())), preferred_element_type=jn...  3.83 us
    concatenate x1, other arithmetic, body(): parts = jnp.concatenate([high, low], axis=1)  2.61 us

profile of v3, /device:TPU:14, one launch (start us, length us, event | category | flops | bytes accessed | tf_op | source)
XLA Modules:
  0.0 113.7 jit_solution(4462468063995491421)
XLA Ops:
  0.0 0.0 copy-start
  0.0 0.9 broadcast_multiply_fusion
  0.9 9.8 %multiply_convert_fusion.refs_2_ = bf16[2048,2048]{1,0:T(8,128)(2,1)} fusion(bf16[2048,2048]{1,0:T(8,128)(2,1)} %param.4, f32[2048]{0:T(1024)S(1)} %get-tuple-element.8, f32[2048]{0:T(1024)S(1)} %get-tuple-element.7), kind=kLoop, calls=%fused_computation | loop fusion | flops 16777216 | bytes 16793600 | tf_op jit(solution)/shard_map/convert_element_type | solution.py:334
  10.7 0.0 copy-done
  10.7 8.2 %fusion = (bf16[2048,512]{1,0:T(8,128)(2,1)S(1)}, bf16[2048,512]{1,0:T(8,128)(2,1)S(1)}) fusion(bf16[2048,2048]{1,0:T(8,128)(2,1)} %multiply_convert_fusion.refs_2_, bf16[2048,512]{1,0:T(8,128)(2,1)S(1)} %copy-done), kind=kOutput, calls=%fused_computation.3 | convolution fusion | flops 4299161600 | bytes 14680064 | tf_op jit(solution)/shard_map/dot_general | solution.py:337
  18.9 1.3 %fusion.3 = f32[512,512]{1,0:T(8,128)S(1)} fusion(bf16[2048,512]{1,0:T(8,128)(2,1)S(1)} %get-tuple-element.6, bf16[2048,512]{1,0:T(8,128)(2,1)S(1)} %get-tuple-element.5), kind=kOutput, calls=%fused_computation.19 | convolution fusion | flops 1073741824 | bytes 5242880 | tf_op jit(solution)/shard_map/dot_general | solution.py:328
  20.2 1.3 %fusion.2 = f32[512,512]{1,0:T(8,128)S(1)} fusion(bf16[2048,512]{1,0:T(8,128)(2,1)S(1)} %get-tuple-element.6), kind=kOutput, calls=%fused_computation.18 | convolution fusion | flops 1073741824 | bytes 3145728 | tf_op jit(solution)/shard_map/dot_general | solution.py:328
  21.4 1.3 %fusion.1 = f32[512,512]{1,0:T(8,128)S(1)} fusion(f32[512,512]{1,0:T(8,128)S(1)} %fusion.2, f32[512,512]{1,0:T(8,128)S(1)} %fusion.3, bf16[2048,512]{1,0:T(8,128)(2,1)S(1)} %get-tuple-element.5, bf16[2048,512]{1,0:T(8,128)(2,1)S(1)} %get-tuple-element.6), kind=kOutput, calls=%fused_computation.6 | convolution fusion | flops 1074266112 | bytes 7340032 | tf_op jit(solution)/shard_map/dot_general | solution.py:328
  22.9 0.0 copy-start.1
  22.9 2.6 %pad_maximum_fusion.refs_3_ = bf16[2048,1024]{1,0:T(8,128)(2,1)} fusion(bf16[2048,512]{1,0:T(8,128)(2,1)S(1)} %get-tuple-element.5, bf16[2048,512]{1,0:T(8,128)(2,1)S(1)} %get-tuple-element.6), kind=kLoop, calls=%fused_computation.4 | loop fusion | flops 8388608 | bytes 8388608 | tf_op jit(solution)/shard_map/concatenate | solution.py:342
  25.5 0.0 copy-done.1
  25.5 86.3 %shard_map.46 = f32[256,512]{1,0:T(8,128)} custom-call(s32[2048]{0:T(1024)} %refs_0_.1, f32[1280,128]{1,0:T(8,128)} %copy-done.1, bf16[2048,2048]{1,0:T(8,128)(2,1)} %multiply_convert_fusion.refs_2_, bf16[2048,1024]{1,0:T(8,128)(2,1)} %pad_maximum_fusion.refs_3_), custom_call_target="tpu_custom_call" | custom-call | tf_op jit(solution)/shard_map/pallas_call | solution.py:287
  111.9 1.9 %copy.17 = f32[256,512]{1,0:T(8,128)} copy(f32[256,512]{1,0:T(8,128)} %shard_map.46) | data formatting | bytes 1048576
  (9 shorter events, 0.1 us)
Async XLA Ops:
  0.0 10.7 %copy-start = (bf16[2048,512]{1,0:T(8,128)(2,1)S(1)}, bf16[2048,512]{1,0:T(8,128)(2,1)}, u32[]{:S(2)}) copy-start(bf16[2048,512]{1,0:T(8,128)(2,1)} %param.6) | copy-start | bytes 6291460
  22.9 2.6 %copy-start.1 = (f32[1280,128]{1,0:T(8,128)}, f32[1280,128]{1,0:T(8,128)S(1)}, u32[]{:S(2)}) copy-start(f32[1280,128]{1,0:T(8,128)S(1)} %slice_dynamic-update-slice_fusion.refs_1_) | copy-start | bytes 1966084
